TPU v7x, 512 devices: a whole 4x4x16 slice. The times are simulated.
512 devices in a mesh: dp: 16 (over z_lo, x), seq: 32 (over z_hi, y, core).
Axes of the slice: x: 4, y: 4, z: 16 (z_hi: 4, z_lo: 4; z = z_hi * 4 + z_lo), core: 2. Of those that a mesh axis runs over, the one named last changes fastest.
Arguments:
- sequence: bfloat16 [262144, 2048], P(('dp', 'seq')), parts along dimension 0, may hold values from -1.5 to 1.5
- norm_gain: float32 [2048], replicated, may hold values from 0.1 to 1.9
- block_factor: bfloat16 [32, 512, 512], P('seq'), may hold values from -0.25 to 0.25
- twiddle: bfloat16 [5, 2, 16384], P(None, None, 'seq'), may hold values from -0.91 to 0.91
- mlp_gain: float32 [2048], replicated, may hold values from 0.1 to 1.9
- gate_weight: bfloat16 [4, 512, 512], P(None, 'seq'), may hold values from -0.25 to 0.25
- up_weight: bfloat16 [4, 512, 512], P(None, 'seq'), may hold values from -0.25 to 0.25
- down_weight: bfloat16 [4, 512, 512], P(None, 'seq'), may hold values from -0.25 to 0.25
Outputs:
- mixed: bfloat16 [262144, 2048], P(('dp', 'seq')), parts along dimension 0
There are 16 independent parts, one for each index of `dp`. A program takes and returns all parts, laid end to end along the dimension named above; an argument that names none is the same for every part. Nothing has to cross between parts.
All inputs are finite; a program needn't handle non-finite values.
Results may differ from a plain program's by a relative error of at most 0.019.
Values may be sent and summed in bfloat16 or wider, within the bound.
A program may use at most 128 MiB of HBM per device.

v0:
```python
import jax
import jax.numpy as jnp
from jax import lax
from jax.sharding import PartitionSpec as P


def swapped(value, axis, stride):
    return lax.ppermute(value, axis, [(i, i ^ 1 << stride) for i in range(lax.axis_size(axis))])


def rms_norm(values, scales):
    floats = values.astype(jnp.float32)
    mean_sq = jnp.mean(floats * floats, axis=-1, keepdims=True)
    return (floats * lax.rsqrt(mean_sq + 1e-06) * scales).astype(jnp.bfloat16)


def local(
    sequence, norm_gain, block_factor, twiddle, mlp_gain, gate_weight, up_weight, down_weight
):
    tok_rows, feat_width = sequence.shape
    seq_count = lax.axis_size("seq")
    level_count = seq_count.bit_length() - 1
    normed = rms_norm(sequence, norm_gain)
    block_here = block_factor.shape[0]
    block_rows = block_factor.shape[1]
    local_mix = jnp.einsum(
        "bij,bjd->bid",
        block_factor,
        normed.reshape(block_here, block_rows, feat_width),
        preferred_element_type=jnp.float32,
    )
    local_mix = local_mix.reshape(tok_rows, feat_width).astype(jnp.bfloat16)
    current = local_mix
    for section_index in range(level_count):
        partner = swapped(current, "seq", section_index)
        own_coef = twiddle[section_index, 0].astype(jnp.float32)[:, None]
        cross_coef = twiddle[section_index, 1].astype(jnp.float32)[:, None]
        current = (
            own_coef * current.astype(jnp.float32) + cross_coef * partner.astype(jnp.float32)
        ).astype(jnp.bfloat16)
    residual = (sequence.astype(jnp.float32) + current.astype(jnp.float32)).astype(jnp.bfloat16)
    normed_two = rms_norm(residual, mlp_gain)
    block_count = gate_weight.shape[0]
    chan_width = feat_width // block_count
    groups = normed_two.reshape(tok_rows, block_count, chan_width)
    slab = groups
    gate_part = jnp.einsum(
        "tkc,kcf->tkf",
        slab,
        lax.all_gather(gate_weight, "seq", axis=1, tiled=True),
        preferred_element_type=jnp.float32,
    )
    up_part = jnp.einsum(
        "tkc,kcf->tkf",
        slab,
        lax.all_gather(up_weight, "seq", axis=1, tiled=True),
        preferred_element_type=jnp.float32,
    )
    hidden = (jax.nn.silu(gate_part) * up_part).astype(jnp.bfloat16)
    slab = hidden
    down_out = jnp.einsum(
        "tkf,kfc->tkc",
        slab,
        lax.all_gather(down_weight, "seq", axis=1, tiled=True),
        preferred_element_type=jnp.float32,
    )
    return (residual.astype(jnp.float32) + down_out.reshape(tok_rows, feat_width)).astype(
        jnp.bfloat16
    )


def solution(mesh):
    return jax.shard_map(
        local,
        mesh=mesh,
        in_specs=(
            P(("dp", "seq"), None),
            P(),
            P("seq", None, None),
            P(None, None, "seq"),
            P(),
            P(None, "seq", None),
            P(None, "seq", None),
            P(None, "seq", None),
        ),
        out_specs=P(("dp", "seq"), None),
        check_vma=False,
    )
```

profile of v0, /device:TPU:1, one launch (start us, length us, event | category | flops | bytes accessed | tf_op | source)
XLA Modules:
  0.0 692.9 jit_solution(11694640076557158037)
XLA Ops:
  6.5 0.0 copy-start
  6.5 0.0 copy-start.6
  6.5 0.0 all-gather.4.cloned.1.call-start
  6.5 2.9 copy.9
  9.5 0.0 copy-start.4
  9.5 0.5 fusion
  10.0 0.0 copy-done
  10.0 0.0 copy-done.6
  10.0 2.6 fusion.12
  12.6 8.8 %collective-permute-start = (bf16[512,2048]{0,1:T(8,128)(2,1)}, bf16[512,2048]{0,1:T(8,128)(2,1)}, u32[]{:S(2)}, u32[]{:S(2)}) collective-permute-start(bf16[512,2048]{0,1:T(8,128)(2,1)} %fusion.12), channel_id=1, source_target_pairs={{0,1},{1,0},{2,3},{3,2},{4,5},{5,4},{6,7},{7,6},{8,9},{9,8},{10,11... | collective-permute-start | bytes 6291464 | tf_op jit(solution)/shard_map/ppermute | solution.py:8
  21.4 0.0 all-gather.4.cloned.1.call-update
  21.5 0.0 all-gather.6.cloned.1.call-start
  21.5 0.0 copy-done.4
  21.5 4.0 collective-permute-done
  25.5 3.0 add_convert_fusion.4
  28.5 1.9 collective-permute-start.1
  30.5 49.5 %collective-permute-done.1 = bf16[512,2048]{0,1:T(8,128)(2,1)S(1)} collective-permute-done((bf16[512,2048]{0,1:T(8,128)(2,1)S(1)}, bf16[512,2048]{0,1:T(8,128)(2,1)S(1)}, u32[]{:S(2)}, u32[]{:S(2)}) %collective-permute-start.1) | collective-permute-done | bytes 2097184 | tf_op jit(solution)/shard_map/ppermute | solution.py:8
  80.0 2.1 add_convert_fusion.3
  82.1 1.9 collective-permute-start.2
  84.0 0.0 all-gather.6.cloned.1.call-update
  84.0 0.0 all-gather.8.cloned.1.call-start
  84.1 48.2 %collective-permute-done.2 = bf16[512,2048]{0,1:T(8,128)(2,1)} collective-permute-done((bf16[512,2048]{0,1:T(8,128)(2,1)}, bf16[512,2048]{0,1:T(8,128)(2,1)}, u32[]{:S(2)}, u32[]{:S(2)}) %collective-permute-start.2) | collective-permute-done | bytes 2097184 | tf_op jit(solution)/shard_map/ppermute | solution.py:8
  132.3 4.3 add_convert_fusion.2
  136.6 6.0 collective-permute-start.3
  142.6 0.0 all-gather.8.cloned.1.call-update
  142.7 232.6 %collective-permute-done.3 = bf16[512,2048]{0,1:T(8,128)(2,1)} collective-permute-done((bf16[512,2048]{0,1:T(8,128)(2,1)}, bf16[512,2048]{0,1:T(8,128)(2,1)}, u32[]{:S(2)}, u32[]{:S(2)}) %collective-permute-start.3) | collective-permute-done | bytes 2097184 | tf_op jit(solution)/shard_map/ppermute | solution.py:8
  375.3 3.0 add_convert_fusion.1
  378.3 11.6 %collective-permute-start.4 = (bf16[512,2048]{0,1:T(8,128)(2,1)S(1)}, bf16[512,2048]{0,1:T(8,128)(2,1)S(1)}, u32[]{:S(2)}, u32[]{:S(2)}) collective-permute-start(bf16[512,2048]{0,1:T(8,128)(2,1)S(1)} %add_convert_fusion.1), channel_id=1, source_target_pairs={{0,16},{1,17},{2,18},{3,19},{4,20},{5,21},{6,22},{7,23},{8,24},{9,... | collective-permute-start | bytes 6291464 | tf_op jit(solution)/shard_map/ppermute | solution.py:8
  389.9 81.9 %collective-permute-done.4 = bf16[512,2048]{0,1:T(8,128)(2,1)S(1)} collective-permute-done((bf16[512,2048]{0,1:T(8,128)(2,1)S(1)}, bf16[512,2048]{0,1:T(8,128)(2,1)S(1)}, u32[]{:S(2)}, u32[]{:S(2)}) %collective-permute-start.4) | collective-permute-done | bytes 2097184 | tf_op jit(solution)/shard_map/ppermute | solution.py:8
  471.8 0.0 copy-start.5
  471.8 1.4 fusion.4
  473.2 0.0 copy-start.1
  473.2 1.3 copy-done.1
  474.5 0.0 copy-done.5
  474.5 0.5 fusion.6
  475.0 0.0 copy-start.3
  475.0 0.0 all-gather.4.cloned.1.call-done
  475.1 1.3 copy-done.3
  476.4 4.9 fusion.20
  481.2 0.0 copy-start.2
  481.2 62.8 %all-gather.6.cloned.1.call-done = bf16[4,512,512]{2,1,0:T(8,128)(2,1)} async-done(((bf16[4,16,512]{2,1,0:T(8,128)(2,1)}), bf16[4,512,512]{2,1,0:T(8,128)(2,1)}) %all-gather.6.cloned.1.call-update) | async-done | bytes 2097168 | tf_op jit(solution)/shard_map/all_gather | solution.py:56
  544.1 125.5 %all-gather.8.cloned.1.call-done = bf16[4,512,512]{2,1,0:T(8,128)(2,1)} async-done(((bf16[4,16,512]{2,1,0:T(8,128)(2,1)}), bf16[4,512,512]{2,1,0:T(8,128)(2,1)}) %all-gather.8.cloned.1.call-update) | async-done | bytes 2097168 | tf_op jit(solution)/shard_map/all_gather | solution.py:64
  669.5 8.7 %fusion.16 = f32[4,512,512]{1,2,0:T(8,128)} fusion(bf16[4,512,512]{2,1,0:T(8,128)(2,1)} %all-gather.8.cloned.1.call-done, f32[4,512,512]{2,1,0:T(8,128)} %fusion.20, bf16[512,4,512]{0,2,1:T(8,128)(2,1)} %bitcast.47, bf16[4,512,512]{2,1,0:T(8,128)(2,1)} %all-gather.6.cloned.1.call-done), kind=kOutput, calls=%fused_computation.30 | convolution fusion | flops 2153775104 | bytes 14680064 | tf_op jit(solution)/shard_map/tkf,kfc->tkc/dot_general | solution.py:61
  678.2 0.0 copy-done.2
  678.2 4.2 fusion.7
  682.5 3.9 copy.11
  (3 shorter events, 0.0 us)
Async XLA Ops:
  6.5 3.5 copy-start
  6.5 3.5 copy-start.6
  6.5 468.5 %all-gather.4.cloned.1.call-start = ((), (), s32[]{:S(2)}) async-start(), calls=%async_computation | async-start | bytes 2162688 | tf_op jit(solution)/shard_map/all_gather | solution.py:50
  9.5 12.0 %copy-start.4 = (bf16[5,2,512]{2,1,0:T(2,128)(2,1)S(1)}, bf16[5,2,512]{2,1,0:T(2,128)(2,1)}, u32[]{:S(2)}) copy-start(bf16[5,2,512]{2,1,0:T(2,128)(2,1)} %param.11) | copy-start | bytes 30724
  12.6 12.9 %collective-permute-start = (bf16[512,2048]{0,1:T(8,128)(2,1)}, bf16[512,2048]{0,1:T(8,128)(2,1)}, u32[]{:S(2)}, u32[]{:S(2)}) collective-permute-start(bf16[512,2048]{0,1:T(8,128)(2,1)} %fusion.12), channel_id=1, source_target_pairs={{0,1},{1,0},{2,3},{3,2},{4,5},{5,4},{6,7},{7,6},{8,9},{9,8},{10,11... | collective-permute-start | bytes 6291464 | tf_op jit(solution)/shard_map/ppermute | solution.py:8
  21.5 522.6 %all-gather.6.cloned.1.call-start = ((), (), s32[]{:S(2)}) async-start(), calls=%async_computation.1 | async-start | bytes 2162688 | tf_op jit(solution)/shard_map/all_gather | solution.py:56
  28.5 51.5 %collective-permute-start.1 = (bf16[512,2048]{0,1:T(8,128)(2,1)S(1)}, bf16[512,2048]{0,1:T(8,128)(2,1)S(1)}, u32[]{:S(2)}, u32[]{:S(2)}) collective-permute-start(bf16[512,2048]{0,1:T(8,128)(2,1)S(1)} %add_convert_fusion.4), channel_id=1, source_target_pairs={{0,2},{1,3},{2,0},{3,1},{4,6},{5,7},{6,4},{7,5},{8,10},{9,11},{10,... | collective-permute-start | bytes 6291464 | tf_op jit(solution)/shard_map/ppermute | solution.py:8
  82.1 50.2 %collective-permute-start.2 = (bf16[512,2048]{0,1:T(8,128)(2,1)}, bf16[512,2048]{0,1:T(8,128)(2,1)}, u32[]{:S(2)}, u32[]{:S(2)}) collective-permute-start(bf16[512,2048]{0,1:T(8,128)(2,1)} %add_convert_fusion.3), channel_id=1, source_target_pairs={{0,4},{1,5},{2,6},{3,7},{4,0},{5,1},{6,2},{7,3},{8,12},{9,13},{10,... | collective-permute-start | bytes 6291464 | tf_op jit(solution)/shard_map/ppermute | solution.py:8
  84.0 585.5 %all-gather.8.cloned.1.call-start = ((), (), s32[]{:S(2)}) async-start(), calls=%async_computation.2 | async-start | bytes 2162688 | tf_op jit(solution)/shard_map/all_gather | solution.py:64
  136.6 238.6 %collective-permute-start.3 = (bf16[512,2048]{0,1:T(8,128)(2,1)}, bf16[512,2048]{0,1:T(8,128)(2,1)}, u32[]{:S(2)}, u32[]{:S(2)}) collective-permute-start(bf16[512,2048]{0,1:T(8,128)(2,1)} %add_convert_fusion.2), channel_id=1, source_target_pairs={{0,8},{1,9},{2,10},{3,11},{4,12},{5,13},{6,14},{7,15},{8,0},{9,1},... | collective-permute-start | bytes 6291464 | tf_op jit(solution)/shard_map/ppermute | solution.py:8
  378.3 93.5 %collective-permute-start.4 = (bf16[512,2048]{0,1:T(8,128)(2,1)S(1)}, bf16[512,2048]{0,1:T(8,128)(2,1)S(1)}, u32[]{:S(2)}, u32[]{:S(2)}) collective-permute-start(bf16[512,2048]{0,1:T(8,128)(2,1)S(1)} %add_convert_fusion.1), channel_id=1, source_target_pairs={{0,16},{1,17},{2,18},{3,19},{4,20},{5,21},{6,22},{7,23},{8,24},{9,... | collective-permute-start | bytes 6291464 | tf_op jit(solution)/shard_map/ppermute | solution.py:8
  471.8 2.7 copy-start.5
  473.2 1.3 copy-start.1
  475.0 1.3 copy-start.3
  481.2 197.0 %copy-start.2 = (bf16[512,2048]{0,1:T(8,128)(2,1)S(1)}, bf16[512,2048]{0,1:T(8,128)(2,1)}, u32[]{:S(2)}) copy-start(bf16[512,2048]{0,1:T(8,128)(2,1)} %copy-done.1) | copy-start | bytes 6291460
Sparse Core Ops, SparseCore 0:
  21.6 78.1 all-gather.3
  103.0 441.0 all-gather.5
  547.2 122.2 all-gather.7
where the time goes:
time: 693 us
  waiting for transfers between devices  605 us (87%)
  starting transfers between devices  30.3 us (4%)
  other arithmetic  19.1 us (3%)
  matrix products  16.2 us (2%)
  between operations  13.2 us (2%)
  local copies, waits for them, and re-layouts  9.45 us (1%)
    ppermute x5, waiting for transfers between devices, swapped(): lax.ppermute(value, axis, [(i, i ^ 1 << stride) for i in range(lax.axis_s...  416 us
    all_gather x1, waiting for transfers between devices, local(): lax.all_gather(down_weight, 'seq', axis=1, tiled=True)  125 us
    all_gather x1, waiting for transfers between devices, local(): lax.all_gather(up_weight, 'seq', axis=1, tiled=True)  62.8 us
    ppermute x5, starting transfers between devices, swapped(): lax.ppermute(value, axis, [(i, i ^ 1 << stride) for i in range(lax.axis_s...  30.2 us
  transfers between devices with their start and end apart: 8, of which 7 were waited for; matrix products, arithmetic and copies ran while one was open for 3% of the time, Pallas kernels for 0%

commit v1 on v0

v1 whole, which is shorter than its diff:
```python
import functools

import jax
import jax.numpy as jnp
from jax import lax
from jax.experimental import pallas as pl
from jax.experimental.pallas import tpu as pltpu
from jax.sharding import PartitionSpec as P

MESH = pl.DeviceIdType.MESH
F32 = jnp.float32
BF16 = jnp.bfloat16

ZH = 4
YN = 4
XN = 4
ROWS = 512
FEAT = 2048
GRP = 512
CH = 8
R = 16
TILE = 512


def flip1(v):
    return v + 1 - 2 * (v % 2)


def flip2(v):
    return v + 2 - 4 * ((v // 2) % 2)


def flips(v):
    return (flip1(v), flip2(v), 3 - v)


def remote(src, dst, send, recv, device):
    return pltpu.make_async_remote_copy(
        src_ref=src,
        dst_ref=dst,
        send_sem=send,
        recv_sem=recv,
        device_id=device,
        device_id_type=MESH,
    )


def kernel(
    seq_hbm,
    ngain_ref,
    bf_hbm,
    tw_ref,
    mgain_ref,
    gw_hbm,
    uw_hbm,
    dw_hbm,
    out_hbm,
    seq,
    bf,
    normed,
    zs,
    z1,
    cr,
    c1,
    y1,
    c2,
    y2,
    ob,
    z2,
    wt,
    tws,
    twr,
    twt,
    xs,
    res,
    outb,
    seq_sem,
    bf_sem,
    w_sem,
    out_sem,
    tw_send,
    tw_recv,
    wz_send,
    wz_recv,
    wy_send,
    wy_recv,
    wx_send,
    wx_recv,
    wc_send,
    wc_recv,
    z1_send,
    z1_recv,
    cr_send,
    cr_recv,
    y1_send,
    y1_recv,
    y2_send,
    y2_recv,
    z2_send,
    z2_recv,
):
    dp = lax.axis_index("dp")
    sq = lax.axis_index("seq")
    zl, xx = dp // XN, dp % XN
    zh, yy, cc = sq // (YN * 2), (sq // 2) % YN, sq % 2

    def place(z=None, y=None, c=None, x=None):
        z = zh if z is None else z
        y = yy if y is None else y
        c = cc if c is None else c
        x = xx if x is None else x
        return (zl * XN + x, z * (YN * 2) + y * 2 + c)

    zp = flips(zh)
    yp = flips(yy)
    xp = flips(xx)
    cp = 1 - cc

    barrier = pltpu.get_barrier_semaphore()
    peers = (
        [place(z=z) for z in zp]
        + [place(y=y) for y in yp]
        + [place(x=x) for x in xp]
        + [place(c=cp)]
    )
    for peer in peers:
        pl.semaphore_signal(barrier, inc=1, device_id=peer, device_id_type=MESH)

    seq_copies = []
    for i in range(4):
        rows = pl.ds(i * 128, 128)
        copy = pltpu.make_async_copy(seq_hbm.at[rows], seq.at[rows], seq_sem.at[i])
        copy.start()
        seq_copies.append(copy)
    bf_copy = pltpu.make_async_copy(bf_hbm.at[0], bf, bf_sem)
    bf_copy.start()
    w_copies = []
    for m, w_hbm in enumerate((gw_hbm, uw_hbm, dw_hbm)):
        copy = pltpu.make_async_copy(
            w_hbm.at[xx], wt.at[xx, zh, yy, cc, pl.ds(m * 16, 16)], w_sem.at[m]
        )
        copy.start()
        w_copies.append(copy)
    for s in range(5):
        tws[pl.ds(2 * s, 2), :] = tw_ref[s].astype(F32)
    tws[pl.ds(10, 6), :] = jnp.zeros((6, ROWS), F32)
    twr[zh] = tws[:, pl.ds(pl.multiple_of(zh * 128, 128), 128)]
    for copy in w_copies:
        copy.wait()

    pl.semaphore_wait(barrier, len(peers))

    wz, tz = [], []
    for i, z in enumerate(zp):
        own = wt.at[xx, zh, yy, cc]
        copy = remote(own, own, wz_send.at[i], wz_recv.at[i], place(z=z))
        copy.start()
        wz.append(copy)
        copy = remote(
            tws.at[:, pl.ds(pl.multiple_of(z * 128, 128), 128)],
            twr.at[zh],
            tw_send.at[i],
            tw_recv.at[i],
            place(z=z),
        )
        copy.start()
        tz.append(copy)

    for i in range(4):
        seq_copies[i].wait()

        @pl.loop(0, 8)
        def _(j):
            rows = pl.ds(pl.multiple_of(i * 128 + j * 16, 16), 16)
            v = seq[rows, :].astype(F32)
            scale = lax.rsqrt(jnp.mean(v * v, axis=-1, keepdims=True) + 1e-6)
            normed[rows, :] = (v * scale * ngain_ref[...]).astype(BF16)

    bf_copy.wait()

    def z1_copy(c, i):
        return remote(
            zs.at[c, zp[i]], z1.at[c, zh], z1_send.at[c, i], z1_recv.at[c, i], place(z=zp[i])
        )

    @pl.loop(0, CH)
    def _(c):
        lhs = jnp.concatenate(
            [bf[pl.ds(pl.multiple_of(q * 128 + c * R, R), R), :] for q in range(ZH)], axis=0
        )
        for n in range(FEAT // TILE):
            cols = pl.ds(n * TILE, TILE)
            mix = jnp.dot(lhs, normed[:, cols], preferred_element_type=F32).astype(BF16)
            zs[c, :, :, cols] = mix.reshape(ZH, R, TILE)
        for i in range(3):
            z1_copy(c, i).start()
        z1[c, zh] = zs[c, zh]

    for copy in wz:
        copy.wait_recv()
    wy = []
    for i, y in enumerate(yp):
        own = wt.at[xx, :, yy, cc]
        copy = remote(own, own, wy_send.at[i], wy_recv.at[i], place(y=y))
        copy.start()
        wy.append(copy)

    for copy in tz:
        copy.wait_recv()
    for z in range(ZH):
        block = jnp.concatenate([twr[z], jnp.zeros((112, 128), F32)], axis=0)
        twt[z] = block.T

    def c_copy(c):
        return remote(z1.at[c], cr.at[c], cr_send.at[c], cr_recv.at[c], place(c=cp))

    def y1_copy(c):
        return remote(c1.at[c], y1.at[c], y1_send.at[c], y1_recv.at[c], place(y=yp[0]))

    def y2_copy(c):
        return remote(c2.at[c], y2.at[c], y2_send.at[c], y2_recv.at[c], place(y=yp[1]))

    def z2_copy(c, i):
        return remote(
            ob.at[c, zp[i]], z2.at[c, zh], z2_send.at[c, i], z2_recv.at[c, i], place(z=zp[i])
        )

    def coefs(c, z, s):
        rows = pl.ds(pl.multiple_of(c * R, R), R)
        block = twt[z, rows, :]
        return block[:, 2 * s : 2 * s + 1], block[:, 2 * s + 1 : 2 * s + 2]

    def section(c, s, cur, other, to):
        for z in range(ZH):
            own, cross = coefs(c, z, s)
            for n in range(FEAT // TILE):
                cols = pl.ds(n * TILE, TILE)
                to[c, z, :, cols] = (
                    own * cur[c, z, :, cols].astype(F32)
                    + cross * other[c, z, :, cols].astype(F32)
                ).astype(BF16)

    def last_sections(c):
        pairs = [[coefs(c, z, s) for z in range(ZH)] for s in (2, 3, 4)]
        for n in range(FEAT // 256):
            cols = pl.ds(n * 256, 256)
            cur = [
                (
                    pairs[0][z][0] * c2[c, z, :, cols].astype(F32)
                    + pairs[0][z][1] * y2[c, z, :, cols].astype(F32)
                )
                .astype(BF16)
                .astype(F32)
                for z in range(ZH)
            ]
            for s, step in ((1, 1), (2, 2)):
                cur = [
                    (pairs[s][z][0] * cur[z] + pairs[s][z][1] * cur[z ^ step])
                    .astype(BF16)
                    .astype(F32)
                    for z in range(ZH)
                ]
            for z in range(ZH):
                ob[c, z, :, cols] = cur[z].astype(BF16)

    @pl.loop(0, CH + 2)
    def _(t):
        @pl.when(t < CH)
        def _():
            for i in range(3):
                z1_copy(t, i).wait_recv()
            c_copy(t).start()

        @pl.when(t >= 2)
        def _():
            c = t - 2
            y2_copy(c).wait_recv()
            last_sections(c)
            for i in range(3):
                z2_copy(c, i).start()
            z2[c, zh] = ob[c, zh]

        @pl.when((t >= 1) & (t < CH + 1))
        def _():
            c = t - 1
            y1_copy(c).wait_recv()
            section(c, 1, c1, y1, c2)
            y2_copy(c).start()

        @pl.when(t < CH)
        def _():
            c_copy(t).wait_recv()
            section(t, 0, z1, cr, c1)
            y1_copy(t).start()

        @pl.when(t == 2)
        def _():
            for i in range(3):
                own = wt.at[xx, :, yy, cc]
                remote(own, own, wy_send.at[i], wy_recv.at[i], place(y=yp[i])).wait_recv()
            for i in range(3):
                own = wt.at[xx, :, :, cc]
                remote(own, own, wx_send.at[i], wx_recv.at[i], place(x=xp[i])).start()

        @pl.when(t == CH + 1)
        def _():
            for i in range(3):
                own = wt.at[xx, :, :, cc]
                remote(own, own, wx_send.at[i], wx_recv.at[i], place(x=xp[i])).wait_recv()
            own = wt.at[:, :, :, cc]
            remote(own, own, wc_send, wc_recv, place(c=cp)).start()

    own = wt.at[:, :, :, cc]
    w_core = remote(own, own, wc_send, wc_recv, place(c=cp))
    w_core.wait_recv()

    def weight(k, m):
        return wt[k, :, :, :, m * 16 : (m + 1) * 16, :].reshape(GRP, GRP)

    def out_copy(c, q):
        rows = pl.ds(pl.multiple_of(q * 128 + c * R, R), R)
        return pltpu.make_async_copy(outb.at[c, q], out_hbm.at[rows], out_sem.at[c, q])

    @pl.loop(0, CH)
    def _(c):
        for i in range(3):
            z2_copy(c, i).wait_recv()
        for q in range(ZH):
            rows = pl.ds(pl.multiple_of(q * 128 + c * R, R), R)
            r = (seq[rows, :].astype(F32) + z2[c, q].astype(F32)).astype(BF16)
            res[pl.ds(q * R, R), :] = r
            v = r.astype(F32)
            scale = lax.rsqrt(jnp.mean(v * v, axis=-1, keepdims=True) + 1e-6)
            xs[pl.ds(q * R, R), :] = (v * scale * mgain_ref[...]).astype(BF16)

        for k in range(FEAT // GRP):
            cols = pl.ds(k * GRP, GRP)
            x = xs[:, cols]
            gate = jnp.dot(x, weight(k, 0), preferred_element_type=F32)
            up = jnp.dot(x, weight(k, 1), preferred_element_type=F32)
            hidden = (gate / (1.0 + jnp.exp(-gate)) * up).astype(BF16)
            down = jnp.dot(hidden, weight(k, 2), preferred_element_type=F32)
            mixed = (res[:, cols].astype(F32) + down).astype(BF16)
            outb[c, :, :, cols] = mixed.reshape(ZH, R, GRP)
        for q in range(ZH):
            out_copy(c, q).start()

    for copy in wz + wy + tz:
        copy.wait_send()
    for i in range(3):
        own = wt.at[xx, :, :, cc]
        remote(own, own, wx_send.at[i], wx_recv.at[i], place(x=xp[i])).wait_send()
    w_core.wait_send()

    @pl.loop(0, CH)
    def _(c):
        for i in range(3):
            z1_copy(c, i).wait_send()
            z2_copy(c, i).wait_send()
        c_copy(c).wait_send()
        y1_copy(c).wait_send()
        y2_copy(c).wait_send()
        for q in range(ZH):
            out_copy(c, q).wait()


def local(
    sequence, norm_gain, block_factor, twiddle, mlp_gain, gate_weight, up_weight, down_weight
):
    any_space = pl.BlockSpec(memory_space=pl.ANY)
    vmem = pl.BlockSpec(memory_space=pltpu.VMEM)
    chunk = pltpu.VMEM((CH, ZH, R, FEAT), BF16)
    dma = pltpu.SemaphoreType.DMA
    return pl.pallas_call(
        kernel,
        name="monarch",
        out_shape=jax.ShapeDtypeStruct((ROWS, FEAT), BF16),
        in_specs=[any_space, vmem, any_space, vmem, vmem, any_space, any_space, any_space],
        out_specs=any_space,
        scratch_shapes=[
            pltpu.VMEM((ROWS, FEAT), BF16),
            pltpu.VMEM((ROWS, ROWS), BF16),
            pltpu.VMEM((ROWS, FEAT), BF16),
            chunk,
            chunk,
            chunk,
            chunk,
            chunk,
            chunk,
            chunk,
            chunk,
            chunk,
            pltpu.VMEM((XN, ZH, YN, 2, 48, GRP), BF16),
            pltpu.VMEM((16, ROWS), F32),
            pltpu.VMEM((ZH, 16, 128), F32),
            pltpu.VMEM((ZH, 128, 128), F32),
            pltpu.VMEM((ZH * R, FEAT), BF16),
            pltpu.VMEM((ZH * R, FEAT), BF16),
            chunk,
            dma((4,)),
            dma,
            dma((3,)),
            dma((CH, ZH)),
            dma((3,)),
            dma((3,)),
            dma((3,)),
            dma((3,)),
            dma((3,)),
            dma((3,)),
            dma((3,)),
            dma((3,)),
            dma,
            dma,
            dma((CH, 3)),
            dma((CH, 3)),
            dma((CH,)),
            dma((CH,)),
            dma((CH,)),
            dma((CH,)),
            dma((CH,)),
            dma((CH,)),
            dma((CH, 3)),
            dma((CH, 3)),
        ],
        compiler_params=pltpu.CompilerParams(
            collective_id=0, has_side_effects=True, vmem_limit_bytes=56 * 1024 * 1024
        ),
        cost_estimate=pl.CostEstimate(
            flops=5 * 2**30, bytes_accessed=8 * 2**20, transcendentals=2**20
        ),
    )(
        sequence,
        norm_gain.reshape(1, FEAT),
        block_factor,
        twiddle,
        mlp_gain.reshape(1, FEAT),
        gate_weight,
        up_weight,
        down_weight,
    )


def solution(mesh):
    return jax.shard_map(
        local,
        mesh=mesh,
        in_specs=(
            P(("dp", "seq"), None),
            P(),
            P("seq", None, None),
            P(None, None, "seq"),
            P(),
            P(None, "seq", None),
            P(None, "seq", None),
            P(None, "seq", None),
        ),
        out_specs=P(("dp", "seq"), None),
        check_vma=False,
    )
```

time: 693 us -> 225 us (0.32)
  the two profiles are of different devices: /device:TPU:1 before, /device:TPU:89 now
where the time goes in v1:
time: 225 us
  Pallas kernels  222 us (99%)
  local copies, waits for them, and re-layouts  3.16 us (1%)
    pallas_call x1, Pallas kernels, local(): pl.pallas_call(kernel, name='monarch', out_shape=jax.ShapeDtypeStruct((RO...  222 us

profile of v1, /device:TPU:89, one launch (start us, length us, event | category | flops | bytes accessed | tf_op | source)
XLA Modules:
  0.0 224.9 jit_solution(7307018566735186529)
XLA Ops:
  0.0 221.7 %monarch.1 = bf16[512,2048]{1,0:T(8,128)(2,1)} custom-call(bf16[512,2048]{1,0:T(8,128)(2,1)} %seq_hbm.1, f32[1,2048]{1,0:T(1,128)} %bitcast.2, bf16[1,512,512]{2,1,0:T(8,128)(2,1)} %bf_hbm.1, bf16[5,2,512]{2,1,0:T(2,128)(2,1)} %tw_ref.1, f32[1,2048]{1,0:T(1,128)} %bitcast.3, bf16[4,16,512]{2,1,0:T(8,128)(2,1)} %gw_hbm.1, bf16[4,16,512]{2,1,0:T(8,128)(2,1)} %uw_hbm.1, ...), custom_call_target="tpu_custom_call" | custom-call | flops 5368709120 | bytes 8388608 | tf_op jit(solution)/shard_map/monarch/pallas_call | solution.py:374
  221.7 3.2 %copy.10 = bf16[512,2048]{1,0:T(8,128)(2,1)} copy(bf16[512,2048]{1,0:T(8,128)(2,1)} %monarch.1) | data formatting | bytes 4194304

commit v2 on v1

--- a/solution.py
+++ b/solution.py
@@ -20,6 +20,7 @@
 CH = 8
 R = 16
 TILE = 512
+YC = 512
 
 
 def flip1(v):
@@ -62,14 +63,14 @@
     z1,
     cr,
     c1,
-    y1,
-    c2,
-    y2,
+    ya,
+    yo,
     ob,
     z2,
     wt,
     tws,
     twr,
+    twy,
     twt,
     xs,
     res,
@@ -80,6 +81,8 @@
     out_sem,
     tw_send,
     tw_recv,
+    ty_send,
+    ty_recv,
     wz_send,
     wz_recv,
     wy_send,
@@ -92,10 +95,10 @@
     z1_recv,
     cr_send,
     cr_recv,
-    y1_send,
-    y1_recv,
-    y2_send,
-    y2_recv,
+    ya_send,
+    ya_recv,
+    yo_send,
+    yo_recv,
     z2_send,
     z2_recv,
 ):
@@ -169,7 +172,7 @@
     for i in range(4):
         seq_copies[i].wait()
 
-        @pl.loop(0, 8)
+        @pl.loop(0, 8, unroll=4)
         def _(j):
             rows = pl.ds(pl.multiple_of(i * 128 + j * 16, 16), 16)
             v = seq[rows, :].astype(F32)
@@ -204,64 +207,79 @@
         copy = remote(own, own, wy_send.at[i], wy_recv.at[i], place(y=y))
         copy.start()
         wy.append(copy)
-
     for copy in tz:
         copy.wait_recv()
-    for z in range(ZH):
-        block = jnp.concatenate([twr[z], jnp.zeros((112, 128), F32)], axis=0)
-        twt[z] = block.T
+    ty = []
+    for i, y in enumerate(yp):
+        copy = remote(twr, twy.at[yy], ty_send.at[i], ty_recv.at[i], place(y=y))
+        copy.start()
+        ty.append(copy)
+    twy[yy] = twr[...]
+    for copy in ty:
+        copy.wait_recv()
+    for h in range(2):
+        twt[h] = twy[2 * h : 2 * h + 2].reshape(128, 128).T
+    twt[2] = jnp.concatenate([twr[...].reshape(64, 128), jnp.zeros((64, 128), F32)], axis=0).T
 
     def c_copy(c):
         return remote(z1.at[c], cr.at[c], cr_send.at[c], cr_recv.at[c], place(c=cp))
 
-    def y1_copy(c):
-        return remote(c1.at[c], y1.at[c], y1_send.at[c], y1_recv.at[c], place(y=yp[0]))
-
-    def y2_copy(c):
-        return remote(c2.at[c], y2.at[c], y2_send.at[c], y2_recv.at[c], place(y=yp[1]))
+    def ya_copy(c, i):
+        cols = pl.ds(pl.multiple_of(yp[i] * YC, YC), YC)
+        return remote(
+            c1.at[c, :, :, cols],
+            ya.at[c, yy],
+            ya_send.at[c, i],
+            ya_recv.at[c, i],
+            place(y=yp[i]),
+        )
+
+    def yo_copy(c, i):
+        cols = pl.ds(pl.multiple_of(yy * YC, YC), YC)
+        return remote(
+            yo.at[c, yp[i]],
+            ob.at[c, :, :, cols],
+            yo_send.at[c, i],
+            yo_recv.at[c, i],
+            place(y=yp[i]),
+        )
 
     def z2_copy(c, i):
         return remote(
             ob.at[c, zp[i]], z2.at[c, zh], z2_send.at[c, i], z2_recv.at[c, i], place(z=zp[i])
         )
 
-    def coefs(c, z, s):
-        rows = pl.ds(pl.multiple_of(c * R, R), R)
-        block = twt[z, rows, :]
-        return block[:, 2 * s : 2 * s + 1], block[:, 2 * s + 1 : 2 * s + 2]
-
-    def section(c, s, cur, other, to):
+    mine = pl.ds(pl.multiple_of(yy * YC, YC), YC)
+
+    def first_section(c):
+        block = twt[2, pl.ds(pl.multiple_of(c * R, R), R), :]
         for z in range(ZH):
-            own, cross = coefs(c, z, s)
+            own, cross = block[:, 16 * z : 16 * z + 1], block[:, 16 * z + 1 : 16 * z + 2]
             for n in range(FEAT // TILE):
                 cols = pl.ds(n * TILE, TILE)
-                to[c, z, :, cols] = (
-                    own * cur[c, z, :, cols].astype(F32)
-                    + cross * other[c, z, :, cols].astype(F32)
+                c1[c, z, :, cols] = (
+                    own * z1[c, z, :, cols].astype(F32) + cross * cr[c, z, :, cols].astype(F32)
                 ).astype(BF16)
 
-    def last_sections(c):
-        pairs = [[coefs(c, z, s) for z in range(ZH)] for s in (2, 3, 4)]
-        for n in range(FEAT // 256):
-            cols = pl.ds(n * 256, 256)
-            cur = [
-                (
-                    pairs[0][z][0] * c2[c, z, :, cols].astype(F32)
-                    + pairs[0][z][1] * y2[c, z, :, cols].astype(F32)
-                )
-                .astype(BF16)
-                .astype(F32)
-                for z in range(ZH)
-            ]
-            for s, step in ((1, 1), (2, 2)):
-                cur = [
-                    (pairs[s][z][0] * cur[z] + pairs[s][z][1] * cur[z ^ step])
-                    .astype(BF16)
-                    .astype(F32)
-                    for z in range(ZH)
-                ]
-            for z in range(ZH):
-                ob[c, z, :, cols] = cur[z].astype(BF16)
+    def other_sections(c):
+        rows = pl.ds(pl.multiple_of(c * R, R), R)
+        blocks = (twt[0, rows, :], twt[1, rows, :])
+
+        def coefs(b, s):
+            lane = (b % 8) * 16 + 2 * s
+            return blocks[b // 8][:, lane : lane + 1], blocks[b // 8][:, lane + 1 : lane + 2]
+
+        for n in range(YC // 128):
+            cols = pl.ds(n * 128, 128)
+            cur = [ya[c, b // ZH, b % ZH, :, cols].astype(F32) for b in range(YN * ZH)]
+            for s, step in ((1, 4), (2, 8), (3, 1), (4, 2)):
+                to = []
+                for b in range(YN * ZH):
+                    own, cross = coefs(b, s)
+                    to.append((own * cur[b] + cross * cur[b ^ step]).astype(BF16))
+                cur = to if s == 4 else [v.astype(F32) for v in to]
+            for b in range(YN * ZH):
+                yo[c, b // ZH, b % ZH, :, cols] = cur[b]
 
     @pl.loop(0, CH + 2)
     def _(t):
@@ -274,8 +292,8 @@
         @pl.when(t >= 2)
         def _():
             c = t - 2
-            y2_copy(c).wait_recv()
-            last_sections(c)
+            for i in range(3):
+                yo_copy(c, i).wait_recv()
             for i in range(3):
                 z2_copy(c, i).start()
             z2[c, zh] = ob[c, zh]
@@ -283,17 +301,22 @@
         @pl.when((t >= 1) & (t < CH + 1))
         def _():
             c = t - 1
-            y1_copy(c).wait_recv()
-            section(c, 1, c1, y1, c2)
-            y2_copy(c).start()
+            for i in range(3):
+                ya_copy(c, i).wait_recv()
+            other_sections(c)
+            for i in range(3):
+                yo_copy(c, i).start()
+            ob[c, :, :, mine] = yo[c, yy]
 
         @pl.when(t < CH)
         def _():
             c_copy(t).wait_recv()
-            section(t, 0, z1, cr, c1)
-            y1_copy(t).start()
-
-        @pl.when(t == 2)
+            first_section(t)
+            for i in range(3):
+                ya_copy(t, i).start()
+            ya[t, yy] = c1[t, :, :, mine]
+
+        @pl.when(t == 1)
         def _():
             for i in range(3):
                 own = wt.at[xx, :, yy, cc]
@@ -302,7 +325,7 @@
                 own = wt.at[xx, :, :, cc]
                 remote(own, own, wx_send.at[i], wx_recv.at[i], place(x=xp[i])).start()
 
-        @pl.when(t == CH + 1)
+        @pl.when(t == 6)
         def _():
             for i in range(3):
                 own = wt.at[xx, :, :, cc]
@@ -345,7 +368,7 @@
         for q in range(ZH):
             out_copy(c, q).start()
 
-    for copy in wz + wy + tz:
+    for copy in wz + wy + tz + ty:
         copy.wait_send()
     for i in range(3):
         own = wt.at[xx, :, :, cc]
@@ -358,8 +381,9 @@
             z1_copy(c, i).wait_send()
             z2_copy(c, i).wait_send()
         c_copy(c).wait_send()
-        y1_copy(c).wait_send()
-        y2_copy(c).wait_send()
+        for i in range(3):
+            ya_copy(c, i).wait_send()
+            yo_copy(c, i).wait_send()
         for q in range(ZH):
             out_copy(c, q).wait()
 
@@ -385,15 +409,15 @@
             chunk,
             chunk,
             chunk,
-            chunk,
-            chunk,
-            chunk,
+            pltpu.VMEM((CH, YN, ZH, R, YC), BF16),
+            pltpu.VMEM((CH, YN, ZH, R, YC), BF16),
             chunk,
             chunk,
             pltpu.VMEM((XN, ZH, YN, 2, 48, GRP), BF16),
             pltpu.VMEM((16, ROWS), F32),
             pltpu.VMEM((ZH, 16, 128), F32),
-            pltpu.VMEM((ZH, 128, 128), F32),
+            pltpu.VMEM((YN, ZH, 16, 128), F32),
+            pltpu.VMEM((3, 128, 128), F32),
             pltpu.VMEM((ZH * R, FEAT), BF16),
             pltpu.VMEM((ZH * R, FEAT), BF16),
             chunk,
@@ -409,16 +433,18 @@
             dma((3,)),
             dma((3,)),
             dma((3,)),
+            dma((3,)),
+            dma((3,)),
             dma,
             dma,
             dma((CH, 3)),
             dma((CH, 3)),
             dma((CH,)),
             dma((CH,)),
-            dma((CH,)),
-            dma((CH,)),
-            dma((CH,)),
-            dma((CH,)),
+            dma((CH, 3)),
+            dma((CH, 3)),
+            dma((CH, 3)),
+            dma((CH, 3)),
             dma((CH, 3)),
             dma((CH, 3)),
         ],

time: 225 us -> 217 us (0.964)
  the two profiles are of different devices: /device:TPU:89 before, /device:TPU:39 now
where the time goes in v2:
time: 217 us; the launch traced here: 216 us
  Pallas kernels  213 us (98%)
  local copies, waits for them, and re-layouts  3.16 us (1%)
    pallas_call x1, Pallas kernels, local(): pl.pallas_call(kernel, name='monarch', out_shape=jax.ShapeDtypeStruct((RO...  213 us

profile of v2, /device:TPU:39, one launch (start us, length us, event | category | flops | bytes accessed | tf_op | source)
XLA Modules:
  0.0 216.2 jit_solution(8197419436541572279)
XLA Ops:
  0.0 213.1 %monarch.1 = bf16[512,2048]{1,0:T(8,128)(2,1)} custom-call(bf16[512,2048]{1,0:T(8,128)(2,1)} %seq_hbm.1, f32[1,2048]{1,0:T(1,128)} %bitcast.2, bf16[1,512,512]{2,1,0:T(8,128)(2,1)} %bf_hbm.1, bf16[5,2,512]{2,1,0:T(2,128)(2,1)} %tw_ref.1, f32[1,2048]{1,0:T(1,128)} %bitcast.3, bf16[4,16,512]{2,1,0:T(8,128)(2,1)} %gw_hbm.1, bf16[4,16,512]{2,1,0:T(8,128)(2,1)} %uw_hbm.1, ...), custom_call_target="tpu_custom_call" | custom-call | flops 5368709120 | bytes 8388608 | tf_op jit(solution)/shard_map/monarch/pallas_call | solution.py:398
  213.1 3.2 %copy.10 = bf16[512,2048]{1,0:T(8,128)(2,1)} copy(bf16[512,2048]{1,0:T(8,128)(2,1)} %monarch.1) | data formatting | bytes 4194304

commit v3 on v2

--- a/solution.py
+++ b/solution.py
@@ -12,6 +12,7 @@
 BF16 = jnp.bfloat16
 
 ZH = 4
+ZL = 4
 YN = 4
 XN = 4
 ROWS = 512
@@ -48,14 +49,17 @@
 
 def kernel(
     seq_hbm,
-    ngain_ref,
+    ngain_hbm,
     bf_hbm,
-    tw_ref,
-    mgain_ref,
+    tw_hbm,
+    mgain_hbm,
     gw_hbm,
     uw_hbm,
     dw_hbm,
     out_hbm,
+    ngain_ref,
+    mgain_ref,
+    tw_ref,
     seq,
     bf,
     normed,
@@ -68,6 +72,7 @@
     ob,
     z2,
     wt,
+    twf,
     tws,
     twr,
     twy,
@@ -77,6 +82,7 @@
     outb,
     seq_sem,
     bf_sem,
+    small_sem,
     w_sem,
     out_sem,
     tw_send,
@@ -85,6 +91,8 @@
     ty_recv,
     wz_send,
     wz_recv,
+    wl_send,
+    wl_recv,
     wy_send,
     wy_recv,
     wx_send,
@@ -114,6 +122,11 @@
         x = xx if x is None else x
         return (zl * XN + x, z * (YN * 2) + y * 2 + c)
 
+    def along(step):
+        z = (zh * ZL + zl + step) % (ZH * ZL)
+        return ((z % ZL) * XN + xx, (z // ZL) * (YN * 2) + sq % (YN * 2))
+
+    piece = pl.ds(pl.multiple_of(zl * 128, 128), 128)
     zp = flips(zh)
     yp = flips(yy)
     xp = flips(xx)
@@ -125,10 +138,18 @@
         + [place(y=y) for y in yp]
         + [place(x=x) for x in xp]
         + [place(c=cp)]
+        + [along(step) for step in (1, ZH * ZL - 1, 2, ZH * ZL - 2)]
     )
     for peer in peers:
         pl.semaphore_signal(barrier, inc=1, device_id=peer, device_id_type=MESH)
 
+    small = []
+    for i, (src, dst) in enumerate(
+        ((tw_hbm, tw_ref), (ngain_hbm, ngain_ref), (mgain_hbm, mgain_ref))
+    ):
+        copy = pltpu.make_async_copy(src, dst, small_sem.at[i])
+        copy.start()
+        small.append(copy)
     seq_copies = []
     for i in range(4):
         rows = pl.ds(i * 128, 128)
@@ -140,22 +161,56 @@
     w_copies = []
     for m, w_hbm in enumerate((gw_hbm, uw_hbm, dw_hbm)):
         copy = pltpu.make_async_copy(
-            w_hbm.at[xx], wt.at[xx, zh, yy, cc, pl.ds(m * 16, 16)], w_sem.at[m]
+            w_hbm.at[xx, :, piece],
+            wt.at[xx, zh, yy, cc, pl.ds(m * 16, 16), piece],
+            w_sem.at[m],
         )
         copy.start()
         w_copies.append(copy)
+    for copy in small:
+        copy.wait()
     for s in range(5):
-        tws[pl.ds(2 * s, 2), :] = tw_ref[s].astype(F32)
-    tws[pl.ds(10, 6), :] = jnp.zeros((6, ROWS), F32)
+        twf[pl.ds(2 * s, 2), :] = tw_ref[s].astype(F32)
+    twf[pl.ds(10, 6), :] = jnp.zeros((6, ROWS), F32)
+    tws[...] = twf[...].astype(BF16)
     twr[zh] = tws[:, pl.ds(pl.multiple_of(zh * 128, 128), 128)]
     for copy in w_copies:
         copy.wait()
 
+    for i in range(4):
+        seq_copies[i].wait()
+
+        @pl.loop(0, 8, unroll=4)
+        def _(j):
+            rows = pl.ds(pl.multiple_of(i * 128 + j * 16, 16), 16)
+            v = seq[rows, :].astype(F32)
+            scale = lax.rsqrt(jnp.mean(v * v, axis=-1, keepdims=True) + 1e-6)
+            normed[rows, :] = (v * scale * ngain_ref[...]).astype(BF16)
+
+    bf_copy.wait()
+
+    def z1_copy(c, i):
+        return remote(
+            zs.at[c, zp[i]], z1.at[c, zh], z1_send.at[c, i], z1_recv.at[c, i], place(z=zp[i])
+        )
+
+    def mix(c):
+        lhs = jnp.concatenate(
+            [bf[pl.ds(pl.multiple_of(q * 128 + c * R, R), R), :] for q in range(ZH)], axis=0
+        )
+        for n in range(FEAT // TILE):
+            cols = pl.ds(n * TILE, TILE)
+            part = jnp.dot(lhs, normed[:, cols], preferred_element_type=F32).astype(BF16)
+            zs[c, :, :, cols] = part.reshape(ZH, R, TILE)
+        z1[c, zh] = zs[c, zh]
+
+    mix(0)
+
     pl.semaphore_wait(barrier, len(peers))
 
     wz, tz = [], []
     for i, z in enumerate(zp):
-        own = wt.at[xx, zh, yy, cc]
+        own = wt.at[xx, zh, yy, cc, :, piece]
         copy = remote(own, own, wz_send.at[i], wz_recv.at[i], place(z=z))
         copy.start()
         wz.append(copy)
@@ -169,44 +224,15 @@
         copy.start()
         tz.append(copy)
 
-    for i in range(4):
-        seq_copies[i].wait()
-
-        @pl.loop(0, 8, unroll=4)
-        def _(j):
-            rows = pl.ds(pl.multiple_of(i * 128 + j * 16, 16), 16)
-            v = seq[rows, :].astype(F32)
-            scale = lax.rsqrt(jnp.mean(v * v, axis=-1, keepdims=True) + 1e-6)
-            normed[rows, :] = (v * scale * ngain_ref[...]).astype(BF16)
-
-    bf_copy.wait()
-
-    def z1_copy(c, i):
-        return remote(
-            zs.at[c, zp[i]], z1.at[c, zh], z1_send.at[c, i], z1_recv.at[c, i], place(z=zp[i])
-        )
-
-    @pl.loop(0, CH)
+    for i in range(3):
+        z1_copy(0, i).start()
+
+    @pl.loop(1, CH)
     def _(c):
-        lhs = jnp.concatenate(
-            [bf[pl.ds(pl.multiple_of(q * 128 + c * R, R), R), :] for q in range(ZH)], axis=0
-        )
-        for n in range(FEAT // TILE):
-            cols = pl.ds(n * TILE, TILE)
-            mix = jnp.dot(lhs, normed[:, cols], preferred_element_type=F32).astype(BF16)
-            zs[c, :, :, cols] = mix.reshape(ZH, R, TILE)
+        mix(c)
         for i in range(3):
             z1_copy(c, i).start()
-        z1[c, zh] = zs[c, zh]
-
-    for copy in wz:
-        copy.wait_recv()
-    wy = []
-    for i, y in enumerate(yp):
-        own = wt.at[xx, :, yy, cc]
-        copy = remote(own, own, wy_send.at[i], wy_recv.at[i], place(y=y))
-        copy.start()
-        wy.append(copy)
+
     for copy in tz:
         copy.wait_recv()
     ty = []
@@ -218,8 +244,29 @@
     for copy in ty:
         copy.wait_recv()
     for h in range(2):
-        twt[h] = twy[2 * h : 2 * h + 2].reshape(128, 128).T
-    twt[2] = jnp.concatenate([twr[...].reshape(64, 128), jnp.zeros((64, 128), F32)], axis=0).T
+        twt[h] = twy[2 * h : 2 * h + 2].astype(F32).reshape(128, 128).T
+    twt[2] = jnp.concatenate([twr[...].astype(F32).reshape(64, 128), jnp.zeros((64, 128), F32)], axis=0).T
+
+    steps = (1, ZH * ZL - 1, 2)
+
+    def z_copy(i):
+        own = wt.at[xx, zh, yy, cc, :, piece]
+        return remote(own, own, wz_send.at[i], wz_recv.at[i], place(z=zp[i]))
+
+    def l_copy(i, got=False):
+        cols = piece
+        if got:
+            cols = pl.ds(pl.multiple_of((zl + 4 * ZL - steps[i]) % ZL * 128, 128), 128)
+        own = wt.at[xx, :, yy, cc, :, cols]
+        return remote(own, own, wl_send.at[i], wl_recv.at[i], along(steps[i]))
+
+    def y_copy(i):
+        own = wt.at[xx, :, yy, cc]
+        return remote(own, own, wy_send.at[i], wy_recv.at[i], place(y=yp[i]))
+
+    def x_copy(i):
+        own = wt.at[xx, :, :, cc]
+        return remote(own, own, wx_send.at[i], wx_recv.at[i], place(x=xp[i]))
 
     def c_copy(c):
         return remote(z1.at[c], cr.at[c], cr_send.at[c], cr_recv.at[c], place(c=cp))
@@ -316,20 +363,31 @@
                 ya_copy(t, i).start()
             ya[t, yy] = c1[t, :, :, mine]
 
-        @pl.when(t == 1)
-        def _():
-            for i in range(3):
-                own = wt.at[xx, :, yy, cc]
-                remote(own, own, wy_send.at[i], wy_recv.at[i], place(y=yp[i])).wait_recv()
-            for i in range(3):
-                own = wt.at[xx, :, :, cc]
-                remote(own, own, wx_send.at[i], wx_recv.at[i], place(x=xp[i])).start()
-
-        @pl.when(t == 6)
-        def _():
-            for i in range(3):
-                own = wt.at[xx, :, :, cc]
-                remote(own, own, wx_send.at[i], wx_recv.at[i], place(x=xp[i])).wait_recv()
+        @pl.when(t == 0)
+        def _():
+            for i in range(3):
+                z_copy(i).wait_recv()
+            for i in range(3):
+                l_copy(i).start()
+
+        @pl.when(t == 2)
+        def _():
+            for i in range(3):
+                l_copy(i, True).wait_recv()
+            for i in range(3):
+                y_copy(i).start()
+
+        @pl.when(t == 3)
+        def _():
+            for i in range(3):
+                y_copy(i).wait_recv()
+            for i in range(3):
+                x_copy(i).start()
+
+        @pl.when(t == 7)
+        def _():
+            for i in range(3):
+                x_copy(i).wait_recv()
             own = wt.at[:, :, :, cc]
             remote(own, own, wc_send, wc_recv, place(c=cp)).start()
 
@@ -368,11 +426,12 @@
         for q in range(ZH):
             out_copy(c, q).start()
 
-    for copy in wz + wy + tz + ty:
+    for copy in wz + tz + ty:
         copy.wait_send()
     for i in range(3):
-        own = wt.at[xx, :, :, cc]
-        remote(own, own, wx_send.at[i], wx_recv.at[i], place(x=xp[i])).wait_send()
+        l_copy(i).wait_send()
+        y_copy(i).wait_send()
+        x_copy(i).wait_send()
     w_core.wait_send()
 
     @pl.loop(0, CH)
@@ -391,17 +450,19 @@
 def local(
     sequence, norm_gain, block_factor, twiddle, mlp_gain, gate_weight, up_weight, down_weight
 ):
-    any_space = pl.BlockSpec(memory_space=pl.ANY)
-    vmem = pl.BlockSpec(memory_space=pltpu.VMEM)
+    hbm = pl.BlockSpec(memory_space=pltpu.HBM)
     chunk = pltpu.VMEM((CH, ZH, R, FEAT), BF16)
     dma = pltpu.SemaphoreType.DMA
     return pl.pallas_call(
         kernel,
         name="monarch",
-        out_shape=jax.ShapeDtypeStruct((ROWS, FEAT), BF16),
-        in_specs=[any_space, vmem, any_space, vmem, vmem, any_space, any_space, any_space],
-        out_specs=any_space,
+        out_shape=pltpu.VMEM((ROWS, FEAT), BF16),
+        in_specs=[hbm] * 8,
+        out_specs=pl.BlockSpec(memory_space=pl.ANY),
         scratch_shapes=[
+            pltpu.VMEM((1, FEAT), F32),
+            pltpu.VMEM((1, FEAT), F32),
+            pltpu.VMEM((5, 2, ROWS), BF16),
             pltpu.VMEM((ROWS, FEAT), BF16),
             pltpu.VMEM((ROWS, ROWS), BF16),
             pltpu.VMEM((ROWS, FEAT), BF16),
@@ -415,8 +476,9 @@
             chunk,
             pltpu.VMEM((XN, ZH, YN, 2, 48, GRP), BF16),
             pltpu.VMEM((16, ROWS), F32),
-            pltpu.VMEM((ZH, 16, 128), F32),
-            pltpu.VMEM((YN, ZH, 16, 128), F32),
+            pltpu.VMEM((16, ROWS), BF16),
+            pltpu.VMEM((ZH, 16, 128), BF16),
+            pltpu.VMEM((YN, ZH, 16, 128), BF16),
             pltpu.VMEM((3, 128, 128), F32),
             pltpu.VMEM((ZH * R, FEAT), BF16),
             pltpu.VMEM((ZH * R, FEAT), BF16),
@@ -424,7 +486,10 @@
             dma((4,)),
             dma,
             dma((3,)),
+            dma((3,)),
             dma((CH, ZH)),
+            dma((3,)),
+            dma((3,)),
             dma((3,)),
             dma((3,)),
             dma((3,)),

time: 217 us -> 211 us (0.972)
  the two profiles are of different devices: /device:TPU:39 before, /device:TPU:1 now
where the time goes in v3:
time: 211 us; the launch traced here: 208 us
  Pallas kernels  207 us (98%)
    pallas_call x1, Pallas kernels, local(): pl.pallas_call(kernel, name='monarch', out_shape=pltpu.VMEM((ROWS, FEAT),...  207 us

profile of v3, /device:TPU:1, one launch (start us, length us, event | category | flops | bytes accessed | tf_op | source)
XLA Modules:
  0.0 208.5 jit_solution(16428797546590528099)
XLA Ops:
  0.0 207.1 %monarch.1 = bf16[512,2048]{1,0:T(8,128)(2,1)S(1)} custom-call(bf16[512,2048]{1,0:T(8,128)(2,1)} %seq_hbm.1, f32[1,2048]{1,0:T(1,128)} %bitcast.2, bf16[1,512,512]{2,1,0:T(8,128)(2,1)} %bf_hbm.1, bf16[5,2,512]{2,1,0:T(2,128)(2,1)} %tw_hbm.1, f32[1,2048]{1,0:T(1,128)} %bitcast.3, bf16[4,16,512]{2,1,0:T(8,128)(2,1)} %gw_hbm.1, bf16[4,16,512]{2,1,0:T(8,128)(2,1)} %uw_hbm.1, ...), custom_call_target="tpu_custom_call" | custom-call | flops 5368709120 | bytes 8388608 | tf_op jit(solution)/shard_map/monarch/pallas_call | solution.py:456
  207.2 1.3 copy.10

commit v4 on v3

--- a/solution.py
+++ b/solution.py
@@ -56,7 +56,7 @@
     gw_hbm,
     uw_hbm,
     dw_hbm,
-    out_hbm,
+    out_ref,
     ngain_ref,
     mgain_ref,
     tw_ref,
@@ -79,12 +79,10 @@
     twt,
     xs,
     res,
-    outb,
     seq_sem,
     bf_sem,
     small_sem,
     w_sem,
-    out_sem,
     tw_send,
     tw_recv,
     ty_send,
@@ -145,7 +143,7 @@
 
     small = []
     for i, (src, dst) in enumerate(
-        ((tw_hbm, tw_ref), (ngain_hbm, ngain_ref), (mgain_hbm, mgain_ref))
+        ((ngain_hbm, ngain_ref), (tw_hbm, tw_ref), (mgain_hbm, mgain_ref))
     ):
         copy = pltpu.make_async_copy(src, dst, small_sem.at[i])
         copy.start()
@@ -167,7 +165,36 @@
         )
         copy.start()
         w_copies.append(copy)
-    for copy in small:
+    small[0].wait()
+    for i in range(4):
+        seq_copies[i].wait()
+
+        @pl.loop(0, 8, unroll=4)
+        def _(j):
+            rows = pl.ds(pl.multiple_of(i * 128 + j * 16, 16), 16)
+            v = seq[rows, :].astype(F32)
+            scale = lax.rsqrt(jnp.mean(v * v, axis=-1, keepdims=True) + 1e-6)
+            normed[rows, :] = (v * scale * ngain_ref[...]).astype(BF16)
+
+    bf_copy.wait()
+
+    def z1_copy(c, i):
+        return remote(
+            zs.at[c, zp[i]], z1.at[c, zh], z1_send.at[c, i], z1_recv.at[c, i], place(z=zp[i])
+        )
+
+    def mix(c):
+        lhs = jnp.concatenate(
+            [bf[pl.ds(pl.multiple_of(q * 128 + c * R, R), R), :] for q in range(ZH)], axis=0
+        )
+        for n in range(FEAT // TILE):
+            cols = pl.ds(n * TILE, TILE)
+            part = jnp.dot(lhs, normed[:, cols], preferred_element_type=F32).astype(BF16)
+            zs[c, :, :, cols] = part.reshape(ZH, R, TILE)
+        z1[c, zh] = zs[c, zh]
+
+    mix(0)
+    for copy in small[1:]:
         copy.wait()
     for s in range(5):
         twf[pl.ds(2 * s, 2), :] = tw_ref[s].astype(F32)
@@ -177,36 +204,9 @@
     for copy in w_copies:
         copy.wait()
 
-    for i in range(4):
-        seq_copies[i].wait()
-
-        @pl.loop(0, 8, unroll=4)
-        def _(j):
-            rows = pl.ds(pl.multiple_of(i * 128 + j * 16, 16), 16)
-            v = seq[rows, :].astype(F32)
-            scale = lax.rsqrt(jnp.mean(v * v, axis=-1, keepdims=True) + 1e-6)
-            normed[rows, :] = (v * scale * ngain_ref[...]).astype(BF16)
-
-    bf_copy.wait()
-
-    def z1_copy(c, i):
-        return remote(
-            zs.at[c, zp[i]], z1.at[c, zh], z1_send.at[c, i], z1_recv.at[c, i], place(z=zp[i])
-        )
-
-    def mix(c):
-        lhs = jnp.concatenate(
-            [bf[pl.ds(pl.multiple_of(q * 128 + c * R, R), R), :] for q in range(ZH)], axis=0
-        )
-        for n in range(FEAT // TILE):
-            cols = pl.ds(n * TILE, TILE)
-            part = jnp.dot(lhs, normed[:, cols], preferred_element_type=F32).astype(BF16)
-            zs[c, :, :, cols] = part.reshape(ZH, R, TILE)
-        z1[c, zh] = zs[c, zh]
-
-    mix(0)
-
     pl.semaphore_wait(barrier, len(peers))
+    for i in range(3):
+        z1_copy(0, i).start()
 
     wz, tz = [], []
     for i, z in enumerate(zp):
@@ -223,9 +223,6 @@
         )
         copy.start()
         tz.append(copy)
-
-    for i in range(3):
-        z1_copy(0, i).start()
 
     @pl.loop(1, CH)
     def _(c):
@@ -328,40 +325,36 @@
             for b in range(YN * ZH):
                 yo[c, b // ZH, b % ZH, :, cols] = cur[b]
 
-    @pl.loop(0, CH + 2)
+    @pl.loop(0, CH + 1)
     def _(t):
         @pl.when(t < CH)
         def _():
             for i in range(3):
                 z1_copy(t, i).wait_recv()
             c_copy(t).start()
-
-        @pl.when(t >= 2)
-        def _():
-            c = t - 2
+            c_copy(t).wait_recv()
+            first_section(t)
+            for i in range(3):
+                ya_copy(t, i).start()
+            ya[t, yy] = c1[t, :, :, mine]
+
+        @pl.when(t >= 1)
+        def _():
+            c = t - 1
             for i in range(3):
                 yo_copy(c, i).wait_recv()
             for i in range(3):
                 z2_copy(c, i).start()
             z2[c, zh] = ob[c, zh]
 
-        @pl.when((t >= 1) & (t < CH + 1))
-        def _():
-            c = t - 1
-            for i in range(3):
-                ya_copy(c, i).wait_recv()
-            other_sections(c)
-            for i in range(3):
-                yo_copy(c, i).start()
-            ob[c, :, :, mine] = yo[c, yy]
-
         @pl.when(t < CH)
         def _():
-            c_copy(t).wait_recv()
-            first_section(t)
-            for i in range(3):
-                ya_copy(t, i).start()
-            ya[t, yy] = c1[t, :, :, mine]
+            for i in range(3):
+                ya_copy(t, i).wait_recv()
+            other_sections(t)
+            for i in range(3):
+                yo_copy(t, i).start()
+            ob[t, :, :, mine] = yo[t, yy]
 
         @pl.when(t == 0)
         def _():
@@ -384,7 +377,7 @@
             for i in range(3):
                 x_copy(i).start()
 
-        @pl.when(t == 7)
+        @pl.when(t == CH)
         def _():
             for i in range(3):
                 x_copy(i).wait_recv()
@@ -397,10 +390,6 @@
 
     def weight(k, m):
         return wt[k, :, :, :, m * 16 : (m + 1) * 16, :].reshape(GRP, GRP)
-
-    def out_copy(c, q):
-        rows = pl.ds(pl.multiple_of(q * 128 + c * R, R), R)
-        return pltpu.make_async_copy(outb.at[c, q], out_hbm.at[rows], out_sem.at[c, q])
 
     @pl.loop(0, CH)
     def _(c):
@@ -422,9 +411,9 @@
             hidden = (gate / (1.0 + jnp.exp(-gate)) * up).astype(BF16)
             down = jnp.dot(hidden, weight(k, 2), preferred_element_type=F32)
             mixed = (res[:, cols].astype(F32) + down).astype(BF16)
-            outb[c, :, :, cols] = mixed.reshape(ZH, R, GRP)
-        for q in range(ZH):
-            out_copy(c, q).start()
+            for q in range(ZH):
+                rows = pl.ds(pl.multiple_of(q * 128 + c * R, R), R)
+                out_ref[rows, cols] = mixed[q * R : (q + 1) * R]
 
     for copy in wz + tz + ty:
         copy.wait_send()
@@ -443,8 +432,6 @@
         for i in range(3):
             ya_copy(c, i).wait_send()
             yo_copy(c, i).wait_send()
-        for q in range(ZH):
-            out_copy(c, q).wait()
 
 
 def local(
@@ -458,7 +445,7 @@
         name="monarch",
         out_shape=pltpu.VMEM((ROWS, FEAT), BF16),
         in_specs=[hbm] * 8,
-        out_specs=pl.BlockSpec(memory_space=pl.ANY),
+        out_specs=pl.BlockSpec(memory_space=pltpu.VMEM),
         scratch_shapes=[
             pltpu.VMEM((1, FEAT), F32),
             pltpu.VMEM((1, FEAT), F32),
@@ -482,12 +469,10 @@
             pltpu.VMEM((3, 128, 128), F32),
             pltpu.VMEM((ZH * R, FEAT), BF16),
             pltpu.VMEM((ZH * R, FEAT), BF16),
-            chunk,
             dma((4,)),
             dma,
             dma((3,)),
             dma((3,)),
-            dma((CH, ZH)),
             dma((3,)),
             dma((3,)),
             dma((3,)),

time: 211 us -> 209 us (level)
  no operation moved by 1% of the time
where the time goes in v4:
time: 209 us; the launch traced here: 208 us
  Pallas kernels  207 us (99%)
    pallas_call x1, Pallas kernels, local(): pl.pallas_call(kernel, name='monarch', out_shape=pltpu.VMEM((ROWS, FEAT),...  207 us

profile of v4, /device:TPU:1, one launch (start us, length us, event | category | flops | bytes accessed | tf_op | source)
XLA Modules:
  0.0 208.1 jit_solution(13905568506808391986)
XLA Ops:
  0.0 206.8 %monarch.1 = bf16[512,2048]{1,0:T(8,128)(2,1)S(1)} custom-call(bf16[512,2048]{1,0:T(8,128)(2,1)} %seq_hbm.1, f32[1,2048]{1,0:T(1,128)} %bitcast.2, bf16[1,512,512]{2,1,0:T(8,128)(2,1)} %bf_hbm.1, bf16[5,2,512]{2,1,0:T(2,128)(2,1)} %tw_hbm.1, f32[1,2048]{1,0:T(1,128)} %bitcast.3, bf16[4,16,512]{2,1,0:T(8,128)(2,1)} %gw_hbm.1, bf16[4,16,512]{2,1,0:T(8,128)(2,1)} %uw_hbm.1, ...), custom_call_target="tpu_custom_call" | custom-call | flops 5368709120 | bytes 8388608 | tf_op jit(solution)/shard_map/monarch/pallas_call | solution.py:443
  206.8 1.3 copy.10

commit v5 on v4

--- a/solution.py
+++ b/solution.py
@@ -125,7 +125,7 @@
         return ((z % ZL) * XN + xx, (z // ZL) * (YN * 2) + sq % (YN * 2))
 
     piece = pl.ds(pl.multiple_of(zl * 128, 128), 128)
-    zp = flips(zh)
+    zp = (flip2(zh), flip1(zh), 3 - zh)
     yp = flips(yy)
     xp = flips(xx)
     cp = 1 - cc
@@ -363,14 +363,14 @@
             for i in range(3):
                 l_copy(i).start()
 
-        @pl.when(t == 2)
+        @pl.when(t == 3)
         def _():
             for i in range(3):
                 l_copy(i, True).wait_recv()
             for i in range(3):
                 y_copy(i).start()
 
-        @pl.when(t == 3)
+        @pl.when(t == 4)
         def _():
             for i in range(3):
                 y_copy(i).wait_recv()

time: 209 us -> 206 us (0.986)
  the two profiles are of different devices: /device:TPU:1 before, /device:TPU:68 now
where the time goes in v5:
time: 206 us
  Pallas kernels  204 us (99%)
    pallas_call x1, Pallas kernels, local(): pl.pallas_call(kernel, name='monarch', out_shape=pltpu.VMEM((ROWS, FEAT),...  204 us

profile of v5, /device:TPU:68, one launch (start us, length us, event | category | flops | bytes accessed | tf_op | source)
XLA Modules:
  0.0 205.6 jit_solution(5183815715824617088)
XLA Ops:
  0.0 204.2 %monarch.1 = bf16[512,2048]{1,0:T(8,128)(2,1)S(1)} custom-call(bf16[512,2048]{1,0:T(8,128)(2,1)} %seq_hbm.1, f32[1,2048]{1,0:T(1,128)} %bitcast.2, bf16[1,512,512]{2,1,0:T(8,128)(2,1)} %bf_hbm.1, bf16[5,2,512]{2,1,0:T(2,128)(2,1)} %tw_hbm.1, f32[1,2048]{1,0:T(1,128)} %bitcast.3, bf16[4,16,512]{2,1,0:T(8,128)(2,1)} %gw_hbm.1, bf16[4,16,512]{2,1,0:T(8,128)(2,1)} %uw_hbm.1, ...), custom_call_target="tpu_custom_call" | custom-call | flops 5368709120 | bytes 8388608 | tf_op jit(solution)/shard_map/monarch/pallas_call | solution.py:443
  204.3 1.3 copy.10
